TPU v7x, 256 devices: a whole 4x4x8 slice. The times are simulated.
256 devices in a mesh: row: 32 (over z, x), col: 8 (over y, core).
Axes of the slice: x: 4, y: 4, z: 8, core: 2. Of those that a mesh axis runs over, the one named last changes fastest.
Arguments:
- features: bfloat16 [32768, 128], P(('col', 'row')), may hold values from -6 to 6
- upstream: bfloat16 [32768, 256], P(('col', 'row')), may hold values from -6 to 6
- tile_values: bfloat16 [32, 8, 192, 128, 128], P('row', 'col'), may hold values from -0.046875 to 0.046875
- tile_rows: int32 [32, 8, 192], P('row', 'col'), may hold values from 0 to 7, as said below
- tile_cols: int32 [32, 8, 192], P('row', 'col'), may hold values from 0 to 31, as said below
- tile_count: int32 [32, 8], P('row', 'col'), may hold values from 48 to 192, as said below
- w_one: bfloat16 [128, 256], replicated, may hold values from -0.5 to 0.5
- b_one: float32 [256], replicated, may hold values from -3 to 3
- w_two: bfloat16 [256, 256], replicated, may hold values from -0.375 to 0.375
- b_two: float32 [256], replicated, may hold values from -3 to 3
Outputs:
- hidden_out: bfloat16 [32768, 256], P(('col', 'row'))
- grad_w_one: float32 [128, 256], replicated
- grad_b_one: float32 [256], replicated
- grad_w_two: float32 [256, 256], replicated
- grad_b_two: float32 [256], replicated
Inputs may be any that keep to these rules, and one draw needn't show every extreme that they name: Within one block the pairs (tile_rows, tile_cols) of all slots are distinct. `tile_cols`: see tile_rows. `tile_count`: some block has all 192 slots live.
All inputs are finite; a program needn't handle non-finite values.
Results may differ from a plain program's by a relative error of at most 0.024.
Values may be sent and summed in bfloat16 or wider, within the bound.
A program may use at most 128 MiB of HBM per device.

v0:
```python
import jax
import jax.numpy as jnp
from jax import lax
from jax.sharding import PartitionSpec as P


def dsilu(value):
    sig = jax.nn.sigmoid(value)
    return sig * (1.0 + value * (1.0 - sig))


def local_forward(values, rows, cols, count, source, row_tiles):
    tile = values.shape[-1]
    width = source.shape[1]
    picked = source.reshape(-1, tile, width)[cols]
    product = jnp.einsum("tab,tbf->taf", values, picked, preferred_element_type=jnp.float32)
    live = jnp.arange(values.shape[0], dtype=jnp.int32) < count
    onehot = (
        (rows[:, None] == jnp.arange(row_tiles, dtype=jnp.int32)[None, :]) & live[:, None]
    ).astype(jnp.float32)
    return jnp.einsum("tr,taf->raf", onehot, product).reshape(row_tiles * tile, width)


def local_backward(values, rows, cols, count, source, col_tiles):
    tile = values.shape[-1]
    width = source.shape[1]
    picked = source.reshape(-1, tile, width)[rows]
    product = jnp.einsum("tab,taf->tbf", values, picked, preferred_element_type=jnp.float32)
    live = jnp.arange(values.shape[0], dtype=jnp.int32) < count
    onehot = (
        (cols[:, None] == jnp.arange(col_tiles, dtype=jnp.int32)[None, :]) & live[:, None]
    ).astype(jnp.float32)
    return jnp.einsum("tc,taf->caf", onehot, product).reshape(col_tiles * tile, width)


def transpose_dot(left, right):
    return lax.dot_general(
        left, right, (((0,), (0,)), ((), ())), preferred_element_type=jnp.float32
    )


def per_device(
    features, upstream, tile_values, tile_rows, tile_cols, tile_count, w_one, b_one, w_two, b_two
):
    values = tile_values[0, 0]
    rows = tile_rows[0, 0]
    cols = tile_cols[0, 0]
    count = tile_count[0, 0]
    tile = values.shape[-1]
    node_rows = features.shape[0]
    row_tiles = node_rows * lax.axis_size("col") // tile
    col_tiles = node_rows * lax.axis_size("row") // tile

    def aggregate(source):
        whole = lax.all_gather(source, "row", axis=0, tiled=True)
        part = local_forward(values, rows, cols, count, whole, row_tiles)
        return lax.psum_scatter(part, "col", scatter_dimension=0, tiled=True)

    agg_in = aggregate(features).astype(jnp.bfloat16)
    pre_one = jnp.dot(agg_in, w_one, preferred_element_type=jnp.float32) + b_one
    hidden_one = jax.nn.silu(pre_one).astype(jnp.bfloat16)
    agg_hidden = aggregate(hidden_one).astype(jnp.bfloat16)
    pre_two = jnp.dot(agg_hidden, w_two, preferred_element_type=jnp.float32) + b_two
    hidden_out = jax.nn.silu(pre_two).astype(jnp.bfloat16)
    grad_two = (upstream.astype(jnp.float32) * dsilu(pre_two)).astype(jnp.bfloat16)
    local_w_two = transpose_dot(agg_hidden, grad_two)
    local_b_two = jnp.sum(grad_two.astype(jnp.float32), axis=0)
    grad_w_two, grad_b_two = lax.psum((local_w_two, local_b_two), ("row", "col"))
    back_two = jnp.dot(grad_two, w_two.T, preferred_element_type=jnp.float32).astype(jnp.bfloat16)
    gathered = lax.all_gather(back_two, "col", axis=0, tiled=True)
    back_part = local_backward(values, rows, cols, count, gathered, col_tiles)
    back_agg = lax.psum_scatter(back_part, "row", scatter_dimension=0, tiled=True)
    grad_one = (back_agg * dsilu(pre_one)).astype(jnp.bfloat16)
    local_w_one = transpose_dot(agg_in, grad_one)
    local_b_one = jnp.sum(grad_one.astype(jnp.float32), axis=0)
    grad_w_one, grad_b_one = lax.psum((local_w_one, local_b_one), ("row", "col"))
    return (hidden_out, grad_w_one, grad_b_one, grad_w_two, grad_b_two)


def solution(mesh):
    in_specs = (
        P(("col", "row"), None),
        P(("col", "row"), None),
        P("row", "col", None, None, None),
        P("row", "col", None),
        P("row", "col", None),
        P("row", "col"),
        P(),
        P(),
        P(),
        P(),
    )
    out_specs = (P(("col", "row"), None), P(), P(), P(), P())
    return jax.shard_map(
        per_device, mesh=mesh, in_specs=in_specs, out_specs=out_specs, check_vma=False
    )
```

profile of v0, /device:TPU:1, one launch (start us, length us, event | category | flops | bytes accessed | tf_op | source)
XLA Modules:
  0.0 860.7 jit_solution(7848495685254805668)
XLA Ops:
  7.2 0.0 copy-start
  7.2 0.0 all-gather.3.cloned.1.call-start
  7.2 0.7 all-gather.3.cloned.1.call-update
  7.9 0.0 reduce-scatter.4.cloned.1.call-start
  8.6 0.7 compare_select_fusion.1
  9.3 76.9 %all-gather.3.cloned.1.call-done = bf16[4096,128]{1,0:T(8,128)(2,1)} async-done(((bf16[128,128]{1,0:T(8,128)(2,1)}), bf16[4096,128]{1,0:T(8,128)(2,1)}) %all-gather.3.cloned.1.call-update) | async-done | bytes 1048592 | tf_op jit(solution)/shard_map/all_gather | solution.py:55
  86.2 9.3 %gather_fusion = bf16[192,128,128]{2,1,0:T(8,128)(2,1)} fusion(bf16[32,128,128]{2,1,0:T(8,128)(2,1)} %bitcast.50, s32[1024]{0:T(1024)S(1)} %pad_clamp_fusion.1), kind=kCustom, calls=%fused_computation | custom fusion | bytes 12583680 | tf_op jit(solution)/shard_map/gather | solution.py:15
  95.5 11.8 %fusion.10 = bf16[192,128,128]{2,1,0:T(8,128)(2,1)} fusion(bf16[192,128,128]{2,1,0:T(8,128)(2,1)} %gather_fusion, bf16[1,1,192,128,128]{4,3,2,1,0:T(8,128)(2,1)} %param.12), kind=kOutput, calls=%fused_computation.13 | convolution fusion | flops 805306368 | bytes 18874368 | tf_op jit(solution)/shard_map/tab,tbf->taf/dot_general | solution.py:16
  107.2 8.9 %copy.19 = bf16[192,128,128]{1,0,2:T(8,128)(2,1)} copy(bf16[192,128,128]{2,1,0:T(8,128)(2,1)} %fusion.10) | data formatting | bytes 12582912 | tf_op jit(solution)/shard_map/tab,tbf->taf/dot_general | solution.py:16
  116.2 3.7 fusion.4
  119.9 0.9 copy.16
  120.8 0.0 reduce-scatter.4.cloned.1.call-update
  120.9 0.0 all-gather.5.cloned.1.call-start
  120.9 33.2 %reduce-scatter.4.cloned.1.call-done = f32[128,128]{1,0:T(8,128)} async-done(((f32[1024,128]{1,0:T(8,128)}), f32[128,128]{1,0:T(8,128)}) %reduce-scatter.4.cloned.1.call-update) | async-done | bytes 65552 | tf_op jit(solution)/shard_map/reduce_scatter | solution.py:57
  154.1 0.0 copy-done.7
  154.1 1.6 multiply_convert_fusion.3
  155.8 0.0 all-gather.5.cloned.1.call-update
  155.8 0.2 reduce-scatter.6.cloned.1.call-start
  156.0 76.8 %all-gather.5.cloned.1.call-done = bf16[4096,256]{1,0:T(8,128)(2,1)} async-done(((bf16[128,256]{1,0:T(8,128)(2,1)}), bf16[4096,256]{1,0:T(8,128)(2,1)}) %all-gather.5.cloned.1.call-update) | async-done | bytes 2097168 | tf_op jit(solution)/shard_map/all_gather | solution.py:55
  232.9 9.8 %gather_fusion.1 = bf16[192,128,256]{2,1,0:T(8,128)(2,1)} fusion(bf16[32,128,256]{2,1,0:T(8,128)(2,1)} %bitcast.49, s32[1024]{0:T(1024)S(1)} %pad_clamp_fusion.1), kind=kCustom, calls=%fused_computation.1 | custom fusion | bytes 25166592 | tf_op jit(solution)/shard_map/gather | solution.py:15
  242.7 10.8 %fusion.8 = bf16[192,256,128]{2,1,0:T(8,128)(2,1)} fusion(bf16[192,128,256]{2,1,0:T(8,128)(2,1)} %gather_fusion.1, bf16[1,1,192,128,128]{4,3,2,1,0:T(8,128)(2,1)} %param.12), kind=kOutput, calls=%fused_computation.11 | convolution fusion | flops 1610612736 | bytes 31457280 | tf_op jit(solution)/shard_map/tab,tbf->taf/dot_general | solution.py:16
  253.5 16.4 %copy.20 = bf16[192,256,128]{1,0,2:T(8,128)(2,1)} copy(bf16[192,256,128]{2,1,0:T(8,128)(2,1)} %fusion.8) | data formatting | bytes 25165824 | tf_op jit(solution)/shard_map/tab,tbf->taf/dot_general | solution.py:16
  269.9 6.3 fusion.2
  276.3 1.3 copy.17
  277.6 0.0 reduce-scatter.6.cloned.1.call-update
  277.6 0.0 reduce-scatter.8.cloned.1.call-start
  277.7 33.3 %reduce-scatter.6.cloned.1.call-done = f32[128,256]{1,0:T(8,128)} async-done(((f32[1024,256]{1,0:T(8,128)}), f32[128,256]{1,0:T(8,128)}) %reduce-scatter.6.cloned.1.call-update) | async-done | bytes 131088 | tf_op jit(solution)/shard_map/reduce_scatter | solution.py:57
  310.9 0.0 copy-done.6
  311.0 1.8 convert_reduce_fusion
  312.7 0.2 convolution_convert_fusion
  312.9 16.2 %all_gather.11 = bf16[1024,256]{1,0:T(8,128)(2,1)S(1)} all-gather(bf16[128,256]{1,0:T(8,128)(2,1)S(1)} %convolution_convert_fusion), channel_id=1, replica_groups=mesh['row'=32,'col'=8] {'col'}, dimensions={0}, use_global_device_ids=true | all-gather | bytes 589824 | tf_op jit(solution)/shard_map/all_gather | solution.py:70
  329.1 8.1 gather_fusion.2
  337.2 11.7 %fusion.6 = bf16[192,256,128]{2,1,0:T(8,128)(2,1)} fusion(bf16[192,128,256]{2,1,0:T(8,128)(2,1)} %gather_fusion.2, bf16[1,1,192,128,128]{4,3,2,1,0:T(8,128)(2,1)} %param.12), kind=kOutput, calls=%fused_computation.9 | convolution fusion | flops 1610612736 | bytes 31457280 | tf_op jit(solution)/shard_map/tab,taf->tbf/dot_general | solution.py:28
  348.9 16.6 %copy.21 = bf16[192,256,128]{1,0,2:T(8,128)(2,1)} copy(bf16[192,256,128]{2,1,0:T(8,128)(2,1)} %fusion.6) | data formatting | bytes 25165824 | tf_op jit(solution)/shard_map/tab,taf->tbf/dot_general | solution.py:28
  365.6 0.0 copy-done.4
  365.6 6.9 fusion
  372.5 4.4 copy.18
  376.9 0.0 reduce-scatter.8.cloned.1.call-update
  376.9 0.0 all-reduce.4.cloned.1.call-start
  377.0 0.9 fusion.12
  377.9 215.1 %reduce-scatter.8.cloned.1.call-done = f32[128,256]{1,0:T(8,128)} async-done(((f32[4096,256]{1,0:T(8,128)}), f32[128,256]{1,0:T(8,128)}) %reduce-scatter.8.cloned.1.call-update) | async-done | bytes 131088 | tf_op jit(solution)/shard_map/reduce_scatter | solution.py:72
  592.9 1.0 convert_reduce_fusion.1
  593.9 0.9 fusion.19
  594.8 0.0 all-reduce.4.cloned.1.call-update
  594.8 79.1 %all-reduce = (f32[256]{0:T(256)}, f32[256]{0:T(256)}) all-reduce(f32[256]{0:T(256)S(1)} %get-tuple-element.11, f32[256]{0:T(256)S(1)} %get-tuple-element.9), channel_id=1, replica_groups=mesh['row'=32,'col'=8] {'row','col'}, use_global_device_ids=true, to_apply=%region_5.6 | all-reduce | flops 512 | bytes 4096 | tf_op jit(solution)/shard_map/psum | solution.py:76
  673.9 176.7 %all-reduce.4.cloned.1.call-done = (f32[128,256]{1,0:T(8,128)}, f32[256,256]{1,0:T(8,128)}) async-done(((f32[128,256]{1,0:T(8,128)}, f32[256,256]{1,0:T(8,128)}), (f32[128,256]{1,0:T(8,128)}, f32[256,256]{1,0:T(8,128)})) %all-reduce.4.cloned.1.call-update) | async-done | bytes 393232 | tf_op jit(solution)/shard_map/psum | solution.py:76
  850.6 1.6 copy.25
  852.2 1.7 copy.26
  (18 shorter events, 0.1 us)
Async XLA Ops:
  7.2 303.8 %copy-start = (bf16[256,256]{1,0:T(8,128)(2,1)S(1)}, bf16[256,256]{1,0:T(8,128)(2,1)}, u32[]{:S(2)}) copy-start(bf16[256,256]{1,0:T(8,128)(2,1)} %param.18) | copy-start | bytes 393220
  7.2 79.0 %all-gather.3.cloned.1.call-start = ((), (), s32[]{:S(2)}) async-start(), calls=%async_computation.3 | async-start | bytes 1081344 | tf_op jit(solution)/shard_map/all_gather | solution.py:55
  7.9 146.2 %reduce-scatter.4.cloned.1.call-start = ((), (), s32[]{:S(2)}) async-start(), calls=%async_computation.4 | async-start | bytes 589824 | tf_op jit(solution)/shard_map/reduce_scatter | solution.py:57
  107.2 8.9 %copy-start.3 = (s32[1,1,192]{2,1,0:T(1,128)S(1)}, s32[1,1,192]{2,1,0:T(1,128)}, u32[]{:S(2)}) copy-start(s32[1,1,192]{2,1,0:T(1,128)} %param.13) | copy-start | bytes 2308
  116.2 38.0 %copy-start.5 = (bf16[128,256]{1,0:T(8,128)(2,1)S(1)}, bf16[128,256]{1,0:T(8,128)(2,1)}, u32[]{:S(2)}) copy-start(bf16[128,256]{1,0:T(8,128)(2,1)} %param.16) | copy-start | bytes 196612
  116.2 38.0 %copy-start.7 = (f32[256]{0:T(256)S(1)}, f32[256]{0:T(256)}, u32[]{:S(2)}) copy-start(f32[256]{0:T(256)} %param.17) | copy-start | bytes 3076
  120.9 112.0 %all-gather.5.cloned.1.call-start = ((), (), s32[]{:S(2)}) async-start(), calls=%async_computation.5 | async-start | bytes 2162688 | tf_op jit(solution)/shard_map/all_gather | solution.py:55
  155.8 155.1 %reduce-scatter.6.cloned.1.call-start = ((), (), s32[]{:S(2)}) async-start(), calls=%async_computation.6 | async-start | bytes 1179648 | tf_op jit(solution)/shard_map/reduce_scatter | solution.py:57
  269.9 41.0 %copy-start.6 = (bf16[128,256]{1,0:T(8,128)(2,1)S(1)}, bf16[128,256]{1,0:T(8,128)(2,1)}, u32[]{:S(2)}) copy-start(bf16[128,256]{1,0:T(8,128)(2,1)} %param.11) | copy-start | bytes 196612
  269.9 41.0 %copy-start.8 = (f32[256]{0:T(256)S(1)}, f32[256]{0:T(256)}, u32[]{:S(2)}) copy-start(f32[256]{0:T(256)} %param.19) | copy-start | bytes 3076
  277.6 315.3 %reduce-scatter.8.cloned.1.call-start = ((), (), s32[]{:S(2)}) async-start(), calls=%async_computation.7 | async-start | bytes 4325376 | tf_op jit(solution)/shard_map/reduce_scatter | solution.py:72
  348.9 16.6 %copy-start.4 = (s32[1,1,192]{2,1,0:T(1,128)S(1)}, s32[1,1,192]{2,1,0:T(1,128)}, u32[]{:S(2)}) copy-start(s32[1,1,192]{2,1,0:T(1,128)} %param.14) | copy-start | bytes 2308
  372.5 4.5 copy-start.1
  372.5 221.4 %copy-start.2 = (f32[128,128]{1,0:T(8,128)S(1)}, f32[128,128]{1,0:T(8,128)}, u32[]{:S(2)}) copy-start(f32[128,128]{1,0:T(8,128)} %reduce-scatter.4.cloned.1.call-done) | copy-start | bytes 196612
  376.9 473.7 %all-reduce.4.cloned.1.call-start = ((), (), s32[]{:S(2)}) async-start(), calls=%async_computation.8 | async-start | bytes 786432 | tf_op jit(solution)/shard_map/psum | solution.py:76
Sparse Core Ops, SparseCore 0:
  10.6 75.5 all-gather.2
  121.0 33.1 reduce-scatter.3
  157.6 75.1 all-gather.4
  277.7 33.1 reduce-scatter.5
  377.0 215.8 reduce-scatter.7
  598.9 251.6 all-reduce.3
where the time goes:
time: 862 us; the launch traced here: 861 us
  waiting for transfers between devices  613 us (71%)
  blocking collectives  95.3 us (11%)
  local copies, waits for them, and re-layouts  79 us (9%)
  matrix products  56.7 us (7%)
  between operations  14.8 us (2%)
    reduce_scatter x1, waiting for transfers between devices, per_device(): lax.psum_scatter(back_part, 'row', scatter_dimension=0, tiled=True)  215 us
    psum x1, waiting for transfers between devices, per_device(): lax.psum((local_w_one, local_b_one), ('row', 'col'))  177 us
    all_gather x2, waiting for transfers between devices, aggregate(): whole = lax.all_gather(source, 'row', axis=0, tiled=True)  154 us
    psum x1, blocking collectives, per_device(): lax.psum((local_w_one, local_b_one), ('row', 'col'))  79.1 us
    reduce_scatter x2, waiting for transfers between devices, aggregate(): return lax.psum_scatter(part, 'col', scatter_dimension=0, tiled=True)  66.5 us
    dot_general x2, local copies, waits for them, and re-layouts, local_forward(): jnp.einsum('tab,tbf->taf', values, picked, preferred_element_type=jnp.flo...  25.4 us
    dot_general x2, matrix products, local_forward(): jnp.einsum('tab,tbf->taf', values, picked, preferred_element_type=jnp.flo...  22.6 us
    gather x2, local copies, waits for them, and re-layouts, local_forward(): picked = source.reshape(-1, tile, width)[cols]  19.1 us
  transfers between devices with their start and end apart: 6, of which 6 were waited for; matrix products, arithmetic and copies ran while one was open for 0% of the time, Pallas kernels for 0%

commit v1 on v0

v1 whole, which is shorter than its diff:
```python
import functools

import jax
import jax.numpy as jnp
from jax import lax
from jax.experimental import pallas as pl
from jax.experimental.pallas import tpu as pltpu
from jax.sharding import PartitionSpec as P

MESH = pl.DeviceIdType.MESH
BF = jnp.bfloat16
F32 = jnp.float32


def dsilu_from(value, sig):
    return sig * (1.0 + value * (1.0 - sig))


def matmul(left, right):
    return jnp.dot(left, right, preferred_element_type=F32)


def wait_for(ref, sem):
    pltpu.make_async_copy(ref, ref, sem).wait()


def send(src, dst, send_sem, recv_sem, **where):
    pltpu.make_async_remote_copy(
        src_ref=src,
        dst_ref=dst,
        send_sem=send_sem,
        recv_sem=recv_sem,
        device_id=where,
        device_id_type=MESH,
    ).start()


def kernel(
    nz, nx, ncol,
    slot_of, features, upstream, tiles_hbm, w_one, b_one, w_two, b_two,
    hidden_out, grad_w_one, grad_b_one, grad_w_two, grad_b_two,
    tiles, dense, dense_t, gath_x, gath_a, agg_t, slope, hid, acc_one, acc_two,
    part_one, land_one, part_two, land_two, back,
    gone, piece_one, land_p1, col_p1, full_p1, piece_two, land_p2, col_p2, full_p2,
    bias_c, bias_x, bias_z, acc_w, acc_b, agg_h, agg_ht, grad_h, local_two,
    tile_sem, ssem, recv_x, recv_a, recv_c, recv_back, recv_w,
):
    nrow = nz * nx
    slots = tiles.shape[0] - 1
    width = features.shape[1]
    hidden = w_one.shape[1]
    half = gath_x.shape[2]
    row = lax.axis_index("row")
    col = lax.axis_index("col")
    mz = row // nx
    mx = lax.rem(row, nx)
    parity = lax.rem(col, 2)

    tile_copy = pltpu.make_async_copy(tiles_hbm.at[0, 0], tiles.at[pl.ds(0, slots)], tile_sem)
    tile_copy.start()
    tiles[slots] = jnp.zeros(tiles.shape[1:], BF)

    barrier = pltpu.get_barrier_semaphore()

    @pl.loop(1, nrow)
    def _(d):
        pl.semaphore_signal(
            barrier, inc=1, device_id={"row": lax.rem(row + d, nrow)}, device_id_type=MESH
        )

    @pl.loop(1, ncol)
    def _(d):
        pl.semaphore_signal(
            barrier, inc=1, device_id={"col": lax.rem(col + d, ncol)}, device_id_type=MESH
        )

    def gather_row(buf, rsem, ssem_, compute, between):
        def push(h, first, count, where):
            part = buf.at[h, pl.ds(first, count)]
            send(part, part, ssem_, rsem.at[h, first], row=where)

        def arrived(h, first, count):
            wait_for(buf.at[h, pl.ds(first, count)], rsem.at[h, first])

        def peer(d):
            return mz * nx + lax.rem(mx + d, nx)

        up = lax.rem(mz + 1, nz) * nx + mx
        down = lax.rem(mz + nz - 1, nz) * nx + mx
        last = nz // 2
        for d in range(1, nx):
            push(1, row, 1, peer(d))

        def onward(h, width_, lower, upper, step):
            if step < last:
                push(h, lower, width_, up)
                push(h, upper, width_, down)
            else:
                push(
                    h,
                    jnp.where(parity == 0, lower, upper),
                    width_,
                    jnp.where(parity == 0, up, down),
                )

        onward(0, 1, row, row, 1)
        for d in range(1, nx):
            push(0, row, 1, peer(d))
        for d in range(1, nx):
            arrived(1, peer(d), 1)
        onward(1, nx, mz * nx, mz * nx, 1)
        ready = [mz]
        for s in range(1, last + 1):
            lower = lax.rem(mz + nz - s, nz)
            upper = lax.rem(mz + s, nz)
            now = [lower, upper] if s < last else [upper]
            for zp in now:
                arrived(0, zp * nx + mx, 1)
            if s < last:
                onward(0, 1, lower * nx + mx, upper * nx + mx, s + 1)
            for zp in now:
                for d in range(1, nx):
                    push(0, zp * nx + mx, 1, peer(d))
            for zp in now:
                arrived(1, zp * nx, nx)
            if s < last:
                onward(1, nx, lower * nx, upper * nx, s + 1)
            if s == 1:
                between()
            for zp in ready:
                for d in range(1, nx):
                    arrived(0, zp * nx + lax.rem(mx + d, nx), 1)
                compute(zp)
            ready = now
        for zp in ready:
            for d in range(1, nx):
                arrived(0, zp * nx + lax.rem(mx + d, nx), 1)
            compute(zp)

    def scatter_col(acc, part, land, rsem, ssem_):
        @pl.loop(1, ncol)
        def _(d):
            to = lax.rem(col + d, ncol)
            part[to] = acc[to].astype(BF)
            send(part.at[to], land.at[col], ssem_, rsem, col=to)

    def scattered_col(acc, land, rsem):
        wait_for(land.at[pl.ds(0, ncol - 1)], rsem)
        total = acc[col]
        for d in range(1, ncol):
            total = total + land[lax.rem(col + d, ncol)].astype(F32)
        return total.astype(BF)

    def build_dense():
        tile_copy.wait()

        @pl.loop(0, nz)
        def _(zp):
            for r in range(ncol):
                for x in range(nx):
                    slot = slot_of[r * nrow + zp * nx + x]
                    dense[zp, pl.ds(r * 128, 128), pl.ds(x * 128, 128)] = tiles[slot]

    rows_step = min(256, ncol * 128)

    def layer_one(zp):
        source = jnp.concatenate(
            [gath_x[h, zp * nx + x] for x in range(nx) for h in range(2)], axis=0
        )

        @pl.loop(0, ncol * 128 // rows_step)
        def _(m):
            at = pl.ds(pl.multiple_of(m * rows_step, rows_step), rows_step)
            more = matmul(dense[zp, at], source).reshape(rows_step // 128, 128, width)
            tiles_at = pl.ds(m * (rows_step // 128), rows_step // 128)
            acc_one[tiles_at] = acc_one[tiles_at] + more

    def layer_two(zp):
        @pl.loop(0, nx)
        def _(x):
            source = jnp.concatenate([gath_a[h, zp * nx + x] for h in range(2)], axis=0)
            pre = matmul(source, w_one[...]) + b_one[...]
            sig = jax.nn.sigmoid(pre)
            at = pl.ds(pl.multiple_of(x * 128, 128), 128)
            slope[zp, at] = dsilu_from(pre, sig)
            hid[at] = (pre * sig).astype(BF)

        @pl.loop(0, ncol * 128 // rows_step)
        def _(m):
            at = pl.ds(pl.multiple_of(m * rows_step, rows_step), rows_step)
            more = matmul(dense[zp, at], hid[...]).reshape(rows_step // 128, 128, hidden)
            tiles_at = pl.ds(m * (rows_step // 128), rows_step // 128)
            acc_two[tiles_at] = acc_two[tiles_at] + more

    def set_own(buf, value):
        buf[0, row] = value[:half]
        buf[1, row] = value[half:]

    set_own(gath_x, features[...])
    acc_one[...] = jnp.zeros(acc_one.shape, F32)
    acc_two[...] = jnp.zeros(acc_two.shape, F32)
    pl.semaphore_wait(barrier, nrow - 1 + ncol - 1)

    gather_row(gath_x, recv_x, ssem.at[0], layer_one, build_dense)

    scatter_col(acc_one, part_one, land_one, recv_c.at[0], ssem.at[1])

    @pl.loop(0, nz)
    def _(zp):
        for r in range(ncol):
            for x in range(nx):
                dense_t[zp, pl.ds(x * 128, 128), pl.ds(r * 128, 128)] = dense[
                    zp, pl.ds(r * 128, 128), pl.ds(x * 128, 128)
                ].T

    set_own(gath_a, scattered_col(acc_one, land_one, recv_c.at[0]))
    gather_row(gath_a, recv_a, ssem.at[2], layer_two, lambda: None)

    scatter_col(acc_two, part_two, land_two, recv_c.at[1], ssem.at[3])

    @pl.loop(0, nz)
    def _(zp):
        for x in range(nx):
            source = jnp.concatenate([gath_a[h, zp * nx + x] for h in range(2)], axis=0)
            agg_t[zp, :, pl.ds(x * 128, 128)] = source.T

    agg_h[...] = scattered_col(acc_two, land_two, recv_c.at[1])

    @pl.loop(0, 2)
    def _(m):
        at = pl.ds(pl.multiple_of(m * 64, 64), 64)
        pre = matmul(agg_h[at], w_two[...]) + b_two[...]
        sig = jax.nn.sigmoid(pre)
        hidden_out[at] = (pre * sig).astype(BF)
        grad = (upstream[at].astype(F32) * dsilu_from(pre, sig)).astype(BF)
        grad_h[at] = grad
        back[pl.ds(pl.multiple_of(col * 128 + m * 64, 64), 64)] = lax.dot_general(
            grad, w_two[...], (((1,), (1,)), ((), ())), preferred_element_type=F32
        ).astype(BF)

    own_back = back.at[pl.ds(pl.multiple_of(col * 128, 128), 128)]

    @pl.loop(1, ncol)
    def _(d):
        send(own_back, own_back, ssem.at[4], recv_back, col=lax.rem(col + d, ncol))

    for m in range(hidden // 128):
        agg_ht[m] = agg_h[:, m * 128 : m * 128 + 128].T

    @pl.loop(0, hidden // 128)
    def _(m):
        local_two[m] = matmul(agg_ht[m], grad_h[...])

    local_w_two = local_two[...].reshape(hidden, hidden)
    local_b_two = jnp.sum(grad_h[...].astype(F32), axis=0, keepdims=True)

    def split_pieces(piece, value):
        per = piece.shape[1] // 8
        for t in range(nrow * per):
            r, c = t // (hidden // 128), t % (hidden // 128)
            piece[t // per, pl.ds((t % per) * 8, 8)] = value[
                r * 8 : r * 8 + 8, c * 128 : c * 128 + 128
            ]

    def join_pieces(piece, out):
        per = piece.shape[1] // 8
        for t in range(nrow * per):
            r, c = t // (hidden // 128), t % (hidden // 128)
            out[pl.ds(r * 8, 8), pl.ds(c * 128, 128)] = piece[t // per, pl.ds((t % per) * 8, 8)]

    def spread_row(piece, land, send_sem, recv_sem):
        @pl.loop(1, nrow)
        def _(d):
            to = lax.rem(row + d, nrow)
            send(piece.at[to], land.at[row], send_sem, recv_sem, row=to)

        land[row] = piece[row]

    def spread_same(buf, send_sem, recv_sem, size, me, axis):
        @pl.loop(1, size)
        def _(d):
            to = lax.rem(me + d, size)
            send(buf.at[me], buf.at[me], send_sem, recv_sem, **{axis: to})

    def total(buf):
        value = buf[0]
        for k in range(1, buf.shape[0]):
            value = value + buf[k]
        return value

    def all_but_one(buf):
        return buf.at[pl.ds(0, buf.shape[0] - 1)]

    split_pieces(piece_two, local_w_two)
    spread_row(piece_two, land_p2, ssem.at[5], recv_w.at[0])
    wait_for(all_but_one(land_p2), recv_w.at[0])
    col_p2[col] = total(land_p2)
    spread_same(col_p2, ssem.at[6], recv_w.at[1], ncol, col, "col")

    wait_for(back.at[pl.ds(0, (ncol - 1) * 128)], recv_back)

    def backward(first, last):
        @pl.loop(first, last)
        def _(zp):
            for p in range(nx * 128 // 256):
                at = pl.ds(p * 256, 256)
                grad_one = (matmul(dense_t[zp, at], back[...]) * slope[zp, at]).astype(BF)
                gone[at] = grad_one
                acc_b[...] = acc_b[...] + jnp.sum(
                    grad_one.astype(F32).reshape(32, 8, hidden), axis=0
                )
            acc_w[...] = acc_w[...] + matmul(agg_t[zp], gone[...])

    acc_w[...] = jnp.zeros(acc_w.shape, F32)
    acc_b[...] = jnp.zeros(acc_b.shape, F32)
    backward(0, nz // 2)
    wait_for(all_but_one(col_p2), recv_w.at[1])
    full_p2[row] = total(col_p2)
    spread_same(full_p2, ssem.at[7], recv_w.at[2], nrow, row, "row")
    backward(nz // 2, nz)

    split_pieces(piece_one, acc_w)
    spread_row(piece_one, land_p1, ssem.at[8], recv_w.at[3])
    local_b_one = jnp.sum(acc_b[...], axis=0, keepdims=True)
    for k, value in enumerate((local_b_one, local_b_two)):
        for c in range(hidden // 128):
            bias_c[col, pl.ds(k * (hidden // 128) + c, 1)] = value[:, c * 128 : c * 128 + 128]
    spread_same(bias_c, ssem.at[9], recv_w.at[4], ncol, col, "col")
    wait_for(all_but_one(land_p1), recv_w.at[3])
    col_p1[col] = total(land_p1)
    spread_same(col_p1, ssem.at[10], recv_w.at[5], ncol, col, "col")
    wait_for(all_but_one(bias_c), recv_w.at[4])
    bias_x[mx] = total(bias_c)

    @pl.loop(1, nx)
    def _(d):
        send(
            bias_x.at[mx], bias_x.at[mx], ssem.at[11], recv_w.at[6],
            row=mz * nx + lax.rem(mx + d, nx),
        )

    wait_for(all_but_one(col_p1), recv_w.at[5])
    full_p1[row] = total(col_p1)
    spread_same(full_p1, ssem.at[12], recv_w.at[7], nrow, row, "row")
    wait_for(all_but_one(bias_x), recv_w.at[6])
    bias_z[mz] = total(bias_x)

    @pl.loop(1, nz)
    def _(d):
        send(
            bias_z.at[mz], bias_z.at[mz], ssem.at[13], recv_w.at[8],
            row=lax.rem(mz + d, nz) * nx + mx,
        )

    wait_for(all_but_one(full_p2), recv_w.at[2])
    join_pieces(full_p2, grad_w_two)
    wait_for(all_but_one(bias_z), recv_w.at[8])
    biases = total(bias_z)
    for k, out in enumerate((grad_b_one, grad_b_two)):
        for c in range(hidden // 128):
            at = k * (hidden // 128) + c
            out[:, pl.ds(c * 128, 128)] = biases[at : at + 1]
    wait_for(all_but_one(full_p1), recv_w.at[7])
    join_pieces(full_p1, grad_w_one)

    wait_for(gath_x.at[:, pl.ds(0, nrow - 1)], ssem.at[0])
    wait_for(all_but_one(part_one), ssem.at[1])
    wait_for(gath_a.at[:, pl.ds(0, nrow - 1)], ssem.at[2])
    wait_for(all_but_one(part_two), ssem.at[3])
    wait_for(back.at[pl.ds(0, (ncol - 1) * 128)], ssem.at[4])
    for k, buf in enumerate(
        (land_p2, col_p2, full_p2, land_p1, bias_c, col_p1, bias_x, full_p1, bias_z)
    ):
        wait_for(all_but_one(buf), ssem.at[5 + k])


def per_device(
    mesh_shape,
    features, upstream, tile_values, tile_rows, tile_cols, tile_count, w_one, b_one, w_two, b_two,
):
    nz, nx, ncol = mesh_shape
    nrow = nz * nx
    slots = tile_values.shape[2]
    width = features.shape[1]
    hidden = w_one.shape[1]
    index = jnp.arange(slots, dtype=jnp.int32)
    place = jnp.where(index < tile_count[0, 0], tile_rows[0, 0] * nrow + tile_cols[0, 0], -1)
    hit = place[None, :] == jnp.arange(ncol * nrow, dtype=jnp.int32)[:, None]
    slot_of = slots + jnp.sum(jnp.where(hit, index[None, :] - slots, 0), axis=1)

    vmem = pl.BlockSpec(memory_space=pltpu.VMEM)
    per_one = width * hidden // (8 * 128) // nrow * 8
    per_two = hidden * hidden // (8 * 128) // nrow * 8
    scratch = [
        pltpu.VMEM((slots + 1, 128, 128), BF),
        pltpu.VMEM((nz, ncol * 128, nx * 128), BF),
        pltpu.VMEM((nz, nx * 128, ncol * 128), BF),
        pltpu.VMEM((2, nrow, 64, width), BF),
        pltpu.VMEM((2, nrow, 64, width), BF),
        pltpu.VMEM((nz, width, nx * 128), BF),
        pltpu.VMEM((nz, nx * 128, hidden), F32),
        pltpu.VMEM((nx * 128, hidden), BF),
        pltpu.VMEM((ncol, 128, width), F32),
        pltpu.VMEM((ncol, 128, hidden), F32),
        pltpu.VMEM((ncol, 128, width), BF),
        pltpu.VMEM((ncol, 128, width), BF),
        pltpu.VMEM((ncol, 128, hidden), BF),
        pltpu.VMEM((ncol, 128, hidden), BF),
        pltpu.VMEM((ncol * 128, hidden), BF),
        pltpu.VMEM((nx * 128, hidden), BF),
        pltpu.VMEM((nrow, per_one, 128), F32),
        pltpu.VMEM((nrow, per_one, 128), F32),
        pltpu.VMEM((ncol, per_one, 128), F32),
        pltpu.VMEM((nrow, per_one, 128), F32),
        pltpu.VMEM((nrow, per_two, 128), F32),
        pltpu.VMEM((nrow, per_two, 128), F32),
        pltpu.VMEM((ncol, per_two, 128), F32),
        pltpu.VMEM((nrow, per_two, 128), F32),
        pltpu.VMEM((ncol, 8, 128), F32),
        pltpu.VMEM((nx, 8, 128), F32),
        pltpu.VMEM((nz, 8, 128), F32),
        pltpu.VMEM((width, hidden), F32),
        pltpu.VMEM((8, hidden), F32),
        pltpu.VMEM((128, hidden), BF),
        pltpu.VMEM((hidden // 128, 128, 128), BF),
        pltpu.VMEM((128, hidden), BF),
        pltpu.VMEM((hidden // 128, 128, hidden), F32),
        pltpu.SemaphoreType.DMA,
        pltpu.SemaphoreType.DMA((14,)),
        pltpu.SemaphoreType.DMA((2, nrow)),
        pltpu.SemaphoreType.DMA((2, nrow)),
        pltpu.SemaphoreType.DMA((2,)),
        pltpu.SemaphoreType.DMA,
        pltpu.SemaphoreType.DMA((9,)),
    ]
    out = pl.pallas_call(
        functools.partial(kernel, nz, nx, ncol),
        out_shape=(
            jax.ShapeDtypeStruct((128, hidden), BF),
            jax.ShapeDtypeStruct((width, hidden), F32),
            jax.ShapeDtypeStruct((1, hidden), F32),
            jax.ShapeDtypeStruct((hidden, hidden), F32),
            jax.ShapeDtypeStruct((1, hidden), F32),
        ),
        in_specs=[
            pl.BlockSpec(memory_space=pltpu.SMEM), vmem, vmem,
            pl.BlockSpec(memory_space=pl.ANY), vmem, vmem, vmem, vmem,
        ],
        out_specs=(vmem,) * 5,
        scratch_shapes=scratch,
        compiler_params=pltpu.CompilerParams(
            collective_id=0, has_side_effects=True, vmem_limit_bytes=56 * 1024 * 1024
        ),
    )(
        slot_of, features, upstream, tile_values, w_one, b_one.reshape(1, hidden),
        w_two, b_two.reshape(1, hidden),
    )
    hidden_out, grad_w_one, grad_b_one, grad_w_two, grad_b_two = out
    return (
        hidden_out, grad_w_one, grad_b_one.reshape(hidden), grad_w_two, grad_b_two.reshape(hidden)
    )


def solution(mesh, nx=4):
    nrow, ncol = mesh.shape["row"], mesh.shape["col"]
    in_specs = (
        P(("col", "row"), None),
        P(("col", "row"), None),
        P("row", "col", None, None, None),
        P("row", "col", None),
        P("row", "col", None),
        P("row", "col"),
        P(),
        P(),
        P(),
        P(),
    )
    out_specs = (P(("col", "row"), None), P(), P(), P(), P())
    return jax.shard_map(
        functools.partial(per_device, (nrow // nx, nx, ncol)),
        mesh=mesh, in_specs=in_specs, out_specs=out_specs, check_vma=False,
    )
```

time: 862 us -> 121 us (0.14)
  waiting for transfers between devices: 613 us -> 0 us
  Pallas kernels: 0 us -> 110 us
  blocking collectives: 95.3 us -> 0 us
  local copies, waits for them, and re-layouts: 79 us -> 7.19 us
  matrix products: 56.7 us -> 0 us
  between operations: 14.8 us -> 1.29 us
    reduce_scatter x3 -> x0, waiting for transfers between devices: 282 us -> none  [the longest x1 215 us: per_device(): lax.psum_scatter(back_part, 'row', scatter_dimension=0, tiled=True)]
    psum x1 -> x0, waiting for transfers between devices: 177 us -> none  [per_device(): lax.psum((local_w_one, local_b_one), ('row', 'col'))]
    all_gather x2 -> x0, waiting for transfers between devices: 154 us -> none  [aggregate(): whole = lax.all_gather(source, 'row', axis=0, tiled=True)]
    pallas_call x0 -> x1, Pallas kernels: none -> 110 us  [per_device(): pl.pallas_call(functools.partial(kernel, nz, nx, ncol), out_shape=(jax.Sh...]
    psum x1 -> x0, blocking collectives: 79.1 us -> none  [per_device(): lax.psum((local_w_one, local_b_one), ('row', 'col'))]
    dot_general x11 -> x0, matrix products: 56.7 us -> none  [the longest x2 22.6 us: local_forward(): jnp.einsum('tab,tbf->taf', values, picked, preferred_element_type=jnp.flo...]
    dot_general x6 -> x0, local copies, waits for them, and re-layouts: 48.6 us -> none  [the longest x2 25.4 us: local_forward(): jnp.einsum('tab,tbf->taf', values, picked, preferred_element_type=jnp.flo...]
    gather x3 -> x0, local copies, waits for them, and re-layouts: 27.1 us -> none  [the longest x2 19.1 us: local_forward(): picked = source.reshape(-1, tile, width)[cols]]
  transfers between devices with their start and end apart: 6 -> 0, of which waited for: 6 -> 0; matrix products, arithmetic and copies ran while one was open for 0% -> 0% of each run, Pallas kernels for 0% -> 0%
where the time goes in v1:
time: 121 us; the launch traced here: 120 us
  Pallas kernels  110 us (91%)
  local copies, waits for them, and re-layouts  7.19 us (6%)
  other arithmetic  1.41 us (1%)
  between operations  1.29 us (1%)
    pallas_call x1, Pallas kernels, per_device(): pl.pallas_call(functools.partial(kernel, nz, nx, ncol), out_shape=(jax.Sh...  110 us
    unnamed x5, local copies, waits for them, and re-layouts  7.19 us

profile of v1, /device:TPU:1, one launch (start us, length us, event | category | flops | bytes accessed | tf_op | source)
XLA Modules:
  0.0 120.3 jit_solution(11386009347444532570)
XLA Ops:
  1.3 0.7 multiply_add_fusion
  2.0 0.1 select_reduce_fusion
  2.1 0.6 broadcast_add_fusion.slot_of
  2.7 110.4 %shard_map.137 = (bf16[128,256]{1,0:T(8,128)(2,1)}, f32[128,256]{1,0:T(8,128)}, f32[1,256]{1,0:T(1,128)}, f32[256,256]{1,0:T(8,128)}, f32[1,256]{1,0:T(1,128)}) custom-call(s32[256]{0:T(256)} %broadcast_add_fusion.slot_of, bf16[128,128]{1,0:T(8,128)(2,1)} %features.1, bf16[128,256]{1,0:T(8,128)(2,1)} %upstream.1, bf16[1,1,192,128,128]{4,3,2,1,0:T(8,128)(2,1)} %tiles_hbm.1, ...), custom_call_target="tpu_custom_call" | custom-call | tf_op jit(solution)/shard_map/pallas_call | solution.py:436
  113.1 1.5 %copy.21 = bf16[128,256]{1,0:T(8,128)(2,1)} copy(bf16[128,256]{1,0:T(8,128)(2,1)} %get-tuple-element.22) | data formatting | bytes 131072
  114.6 1.6 %copy.22 = f32[128,256]{1,0:T(8,128)} copy(f32[128,256]{1,0:T(8,128)} %get-tuple-element.23) | data formatting | bytes 262144
  116.2 1.2 %copy.23 = f32[256]{0:T(256)} copy(f32[256]{0:T(256)} %bitcast.11) | data formatting | bytes 2048
  117.4 1.7 %copy.24 = f32[256,256]{1,0:T(8,128)} copy(f32[256,256]{1,0:T(8,128)} %get-tuple-element.25) | data formatting | bytes 524288
  119.1 1.2 %copy.25 = f32[256]{0:T(256)} copy(f32[256]{0:T(256)} %bitcast.10) | data formatting | bytes 2048
  (1 shorter events, 0.0 us)

commit v2 on v1

v2 whole, which is shorter than its diff:
```python
import functools

import jax
import jax.numpy as jnp
from jax import lax
from jax.experimental import pallas as pl
from jax.experimental.pallas import tpu as pltpu
from jax.sharding import PartitionSpec as P

MESH = pl.DeviceIdType.MESH
BF = jnp.bfloat16
F32 = jnp.float32


def dsilu_from(value, sig):
    return sig * (1.0 + value * (1.0 - sig))


def matmul(left, right):
    return jnp.dot(left, right, preferred_element_type=F32)


def wait_for(ref, sem):
    pltpu.make_async_copy(ref, ref, sem).wait()


def send(src, dst, send_sem, recv_sem, **where):
    pltpu.make_async_remote_copy(
        src_ref=src,
        dst_ref=dst,
        send_sem=send_sem,
        recv_sem=recv_sem,
        device_id=where,
        device_id_type=MESH,
    ).start()


def kernel(
    nz, nx, ncol,
    count, features, upstream_hbm, tiles_hbm, rows_hbm, cols_hbm,
    w_one_hbm, b_one_hbm, w_two_hbm, b_two_hbm,
    hidden_out, grad_w_one, grad_b_one, grad_w_two, grad_b_two,
    tiles, dense, dense_t, gz_x, gx_x, gz_a, gx_a, agg_t, slope, hid, acc_one, acc_two,
    part_one, land_one, part_two, land_two, back,
    gone, piece_one, land_p1, z_p1, full_p1, piece_two, land_p2, z_p2, full_p2,
    bias_c, bias_x, bias_z, acc_w, acc_b, agg_h, agg_ht, grad_h, local_two,
    upstream, w_one, b_one, w_two, b_two, rows_of, cols_of, slots_vmem, slot_of,
    tile_sem, in_sem, ssem, recv_x, recv_a, recv_c, recv_back, recv_w,
):
    nrow = nz * nx
    slots = tiles.shape[0] - 1
    width = features.shape[1]
    hidden = w_one.shape[1]
    far_first = [nz // 2] + [d * g for d in range(nz // 2 - 1, 0, -1) for g in (1, -1)]
    row = lax.axis_index("row")
    col = lax.axis_index("col")
    mz = row // nx
    mx = lax.rem(row, nx)
    group = mx * ncol + col
    ngroup = nx * ncol
    cut = gz_x.shape[1]

    tile_copy = pltpu.make_async_copy(tiles_hbm.at[0, 0], tiles.at[pl.ds(0, slots)], tile_sem)
    own_copies = [
        pltpu.make_async_copy(src, dst, in_sem.at[k])
        for k, (src, dst) in enumerate((
            (rows_hbm.at[0], rows_of),
            (cols_hbm.at[0], cols_of),
            (features.at[pl.ds(0, cut)], gz_x.at[row]),
            (features.at[pl.ds(cut, 128 - cut)], gx_x.at[row]),
            (w_one_hbm, w_one),
            (b_one_hbm, b_one),
            (w_two_hbm, w_two),
            (b_two_hbm, b_two),
            (upstream_hbm, upstream),
        ))
    ]
    for copy in own_copies:
        copy.start()
    tile_copy.start()

    barrier = pltpu.get_barrier_semaphore()

    def member(d):
        to = lax.rem(group + d, ngroup)
        return to, {"row": mz * nx + to // ncol, "col": lax.rem(to, ncol)}

    @pl.loop(1, nz)
    def _(d):
        pl.semaphore_signal(
            barrier, inc=1, device_id={"row": lax.rem(mz + d, nz) * nx + mx}, device_id_type=MESH
        )

    @pl.loop(1, ngroup)
    def _(d):
        pl.semaphore_signal(barrier, inc=1, device_id=member(d)[1], device_id_type=MESH)

    def peer_x(d):
        return lax.rem(mx + d, nx)

    def peer_z(d):
        return lax.rem(mz + d + nz, nz)

    def gather_row(by_z, by_x, own_z, own_x, rsem, ssem_, compute, placed, between):
        def push(buf, sems, first, number, z, x):
            part = buf.at[pl.ds(first, number)]
            send(part, part, ssem_, sems.at[first], row=z * nx + x)

        def push_own(buf, own, sems, z, x):
            send(own, buf.at[row], ssem_, sems.at[row], row=z * nx + x)

        def arrived(buf, sems, first, number):
            wait_for(buf.at[pl.ds(first, number)], sems.at[first])

        sems_z, sems_x = rsem.at[0], rsem.at[1]
        for d in range(1, nx):
            push_own(by_x, own_x, sems_x, mz, peer_x(d))
        for d in far_first[::-1]:
            push_own(by_z, own_z, sems_z, peer_z(d), mx)
        for d in range(1, nx):
            push_own(by_z, own_z, sems_z, mz, peer_x(d))
        placed()
        for d in range(1, nx):
            arrived(by_x, sems_x, mz * nx + peer_x(d), 1)
        for d in far_first[::-1]:
            push(by_x, sems_x, mz * nx, nx, peer_z(d), mx)

        def onward(d):
            at = peer_z(d) * nx + mx
            arrived(by_z, sems_z, at, 1)
            for e in range(1, nx):
                push(by_z, sems_z, at, 1, mz, peer_x(e))

        def use(d):
            for e in range(1, nx):
                arrived(by_z, sems_z, peer_z(d) * nx + peer_x(e), 1)
            if d:
                arrived(by_x, sems_x, peer_z(d) * nx, nx)
            compute(peer_z(d))

        between()
        near_first = far_first[::-1]
        early = len(near_first) // 2 + 1
        for d in near_first[:early]:
            onward(d)
        use(0)
        for d in near_first[early:]:
            onward(d)
        for d in near_first:
            use(d)

    def scatter_col(acc, part, land, rsem, ssem_):
        @pl.loop(1, ncol)
        def _(d):
            to = lax.rem(col + d, ncol)
            part[to] = acc[to].astype(BF)
            send(part.at[to], land.at[col], ssem_, rsem, col=to)

    def scattered_col(acc, land, rsem):
        wait_for(land.at[pl.ds(0, ncol - 1)], rsem)
        total = acc[col]
        for d in range(1, ncol):
            total = total + land[lax.rem(col + d, ncol)].astype(F32)
        return total.astype(BF)

    def own_placed():
        own_copies[2].wait()
        own_copies[3].wait()

    def find_slots():
        own_copies[0].wait()
        own_copies[1].wait()
        places = ncol * nrow
        index = lax.broadcasted_iota(jnp.int32, (1, slots), 1)
        place = jnp.where(index < count[0, 0], rows_of[...] * nrow + cols_of[...], -1)
        column = jnp.broadcast_to(place, (8, slots)).T[:, :1]
        hit = column == lax.broadcasted_iota(jnp.int32, (slots, places), 1)
        entry = lax.broadcasted_iota(jnp.int32, (slots, places), 0) - slots
        found = jnp.sum(jnp.where(hit, entry, 0), axis=0, keepdims=True) + slots
        slots_vmem[...] = jnp.broadcast_to(found, slots_vmem.shape)
        to_smem = pltpu.make_async_copy(slots_vmem, slot_of, in_sem.at[0])
        to_smem.start()
        tiles[slots] = jnp.zeros(tiles.shape[1:], BF)
        acc_one[...] = jnp.zeros(acc_one.shape, F32)
        acc_two[...] = jnp.zeros(acc_two.shape, F32)
        for copy in own_copies[4:]:
            copy.wait()
        to_smem.wait()
        tile_copy.wait()

    def build_dense(zp):
        for r in range(ncol):
            for x in range(nx):
                slot = jnp.clip(slot_of[0, r * nrow + zp * nx + x], 0, slots)
                dense[zp, pl.ds(r * 128, 128), pl.ds(x * 128, 128)] = tiles[slot]

    rows_step = min(1024, ncol * 128)

    def layer_one(zp):
        build_dense(zp)
        source = jnp.concatenate(
            [buf[zp * nx + x] for x in range(nx) for buf in (gz_x, gx_x)], axis=0
        )

        @pl.loop(0, ncol * 128 // rows_step)
        def _(m):
            at = pl.ds(pl.multiple_of(m * rows_step, rows_step), rows_step)
            more = matmul(dense[zp, at], source).reshape(rows_step // 128, 128, width)
            tiles_at = pl.ds(m * (rows_step // 128), rows_step // 128)
            acc_one[tiles_at] = acc_one[tiles_at] + more

    def layer_two(zp):
        for x in range(nx):
            source = jnp.concatenate([gz_a[zp * nx + x], gx_a[zp * nx + x]], axis=0)
            pre = matmul(source, w_one[...]) + b_one[...]
            sig = jax.nn.sigmoid(pre)
            at = pl.ds(x * 128, 128)
            slope[zp, at] = dsilu_from(pre, sig)
            hid[at] = (pre * sig).astype(BF)

        @pl.loop(0, ncol * 128 // rows_step)
        def _(m):
            at = pl.ds(pl.multiple_of(m * rows_step, rows_step), rows_step)
            more = matmul(dense[zp, at], hid[...]).reshape(rows_step // 128, 128, hidden)
            tiles_at = pl.ds(m * (rows_step // 128), rows_step // 128)
            acc_two[tiles_at] = acc_two[tiles_at] + more

    def set_own(by_z, by_x, value):
        by_z[row] = value[:cut]
        by_x[row] = value[cut:]

    pl.semaphore_wait(barrier, nz - 1 + ngroup - 1)

    gather_row(
        gz_x, gx_x, features.at[pl.ds(0, cut)], features.at[pl.ds(cut, 128 - cut)],
        recv_x, ssem.at[0], layer_one, own_placed, find_slots,
    )


    scatter_col(acc_one, part_one, land_one, recv_c.at[0], ssem.at[1])

    @pl.loop(0, nz)
    def _(zp):
        for r in range(ncol):
            for x in range(nx):
                dense_t[zp, pl.ds(x * 128, 128), pl.ds(r * 128, 128)] = dense[
                    zp, pl.ds(r * 128, 128), pl.ds(x * 128, 128)
                ].T

    set_own(gz_a, gx_a, scattered_col(acc_one, land_one, recv_c.at[0]))

    gather_row(
        gz_a, gx_a, gz_a.at[row], gx_a.at[row], recv_a, ssem.at[2], layer_two,
        lambda: None, lambda: None,
    )


    scatter_col(acc_two, part_two, land_two, recv_c.at[1], ssem.at[3])

    @pl.loop(0, nz)
    def _(zp):
        for x in range(nx):
            source = jnp.concatenate([gz_a[zp * nx + x], gx_a[zp * nx + x]], axis=0)
            agg_t[zp, :, pl.ds(x * 128, 128)] = source.T

    agg_h[...] = scattered_col(acc_two, land_two, recv_c.at[1])

    @pl.loop(0, 2)
    def _(m):
        at = pl.ds(pl.multiple_of(m * 64, 64), 64)
        pre = matmul(agg_h[at], w_two[...]) + b_two[...]
        sig = jax.nn.sigmoid(pre)
        hidden_out[at] = (pre * sig).astype(BF)
        grad = (upstream[at].astype(F32) * dsilu_from(pre, sig)).astype(BF)
        grad_h[at] = grad
        back[pl.ds(pl.multiple_of(col * 128 + m * 64, 64), 64)] = lax.dot_general(
            grad, w_two[...], (((1,), (1,)), ((), ())), preferred_element_type=F32
        ).astype(BF)

    own_back = back.at[pl.ds(pl.multiple_of(col * 128, 128), 128)]

    @pl.loop(1, ncol)
    def _(d):
        send(own_back, own_back, ssem.at[4], recv_back, col=lax.rem(col + d, ncol))

    for m in range(hidden // 128):
        agg_ht[m] = agg_h[:, m * 128 : m * 128 + 128].T

    @pl.loop(0, hidden // 128)
    def _(m):
        local_two[m] = matmul(agg_ht[m], grad_h[...])

    local_w_two = local_two[...].reshape(hidden, hidden)
    local_b_two = jnp.sum(grad_h[...].astype(F32), axis=0, keepdims=True)

    def tile_places(per):
        for t in range(ngroup * per // 8):
            r, c = t // (hidden // 128), t % (hidden // 128)
            yield t // (per // 8), pl.ds(t % (per // 8) * 8, 8), slice(r * 8, r * 8 + 8), slice(c * 128, c * 128 + 128)

    def split_pieces(piece, value):
        for n, at, r, c in tile_places(piece.shape[1]):
            piece[n, at] = value[r, c].astype(piece.dtype)

    def join_pieces(piece, out):
        for n, at, r, c in tile_places(piece.shape[1]):
            out[r, c] = piece[n, at]

    def spread_group(piece, land, send_sem, recv_sem):
        @pl.loop(1, ngroup)
        def _(d):
            to, where = member(d)
            send(piece.at[to], land.at[group], send_sem, recv_sem, **where)

        land[group] = piece[group]

    def gather_group(buf, send_sem, recv_sem):
        @pl.loop(1, ngroup)
        def _(d):
            send(buf.at[group], buf.at[group], send_sem, recv_sem, **member(d)[1])

    def share(buf, send_sem, recv_sem, me, where):
        @pl.loop(1, buf.shape[0])
        def _(d):
            send(
                buf.at[me], buf.at[me], send_sem, recv_sem,
                **where(lax.rem(me + d, buf.shape[0])),
            )

    def along_z(z):
        return {"row": z * nx + mx}

    def along_x(x):
        return {"row": mz * nx + x}

    def along_col(c):
        return {"col": c}

    def total(buf):
        value = buf[0].astype(F32)
        for k in range(1, buf.shape[0]):
            value = value + buf[k].astype(F32)
        return value

    def all_but_one(buf):
        return buf.at[pl.ds(0, buf.shape[0] - 1)]

    split_pieces(piece_two, local_w_two)
    spread_group(piece_two, land_p2, ssem.at[5], recv_w.at[0])

    wait_for(back.at[pl.ds(0, (ncol - 1) * 128)], recv_back)

    def backward(first, last):
        @pl.loop(first, last)
        def _(zp):
            for p in range(1):
                at = pl.ds(0, nx * 128)
                grad_one = (matmul(dense_t[zp, at], back[...]) * slope[zp, at]).astype(BF)
                gone[at] = grad_one
                acc_b[...] = acc_b[...] + jnp.sum(
                    grad_one.astype(F32).reshape(nx * 16, 8, hidden), axis=0
                )
            acc_w[...] = acc_w[...] + matmul(agg_t[zp], gone[...])

    acc_w[...] = jnp.zeros(acc_w.shape, F32)
    acc_b[...] = jnp.zeros(acc_b.shape, F32)
    backward(0, nz // 2)
    wait_for(all_but_one(land_p2), recv_w.at[0])
    z_p2[mz] = total(land_p2)
    share(z_p2, ssem.at[6], recv_w.at[1], mz, along_z)
    backward(nz // 2, nz)

    split_pieces(piece_one, acc_w)
    spread_group(piece_one, land_p1, ssem.at[7], recv_w.at[2])
    local_b_one = jnp.sum(acc_b[...], axis=0, keepdims=True)
    for k, value in enumerate((local_b_one, local_b_two)):
        for c in range(hidden // 128):
            bias_z[mz, pl.ds(k * (hidden // 128) + c, 1)] = value[:, c * 128 : c * 128 + 128]
    share(bias_z, ssem.at[8], recv_w.at[3], mz, along_z)
    wait_for(all_but_one(z_p2), recv_w.at[1])
    full_p2[group] = total(z_p2)
    gather_group(full_p2, ssem.at[9], recv_w.at[4])

    wait_for(all_but_one(land_p1), recv_w.at[2])
    z_p1[mz] = total(land_p1)
    share(z_p1, ssem.at[10], recv_w.at[5], mz, along_z)
    wait_for(all_but_one(bias_z), recv_w.at[3])
    bias_x[mx] = total(bias_z)
    share(bias_x, ssem.at[11], recv_w.at[6], mx, along_x)

    wait_for(all_but_one(full_p2), recv_w.at[4])
    join_pieces(full_p2, grad_w_two)

    wait_for(all_but_one(z_p1), recv_w.at[5])
    full_p1[group] = total(z_p1)
    gather_group(full_p1, ssem.at[12], recv_w.at[7])
    wait_for(all_but_one(bias_x), recv_w.at[6])
    bias_c[col] = total(bias_x)
    share(bias_c, ssem.at[13], recv_w.at[8], col, along_col)

    wait_for(all_but_one(bias_c), recv_w.at[8])
    biases = total(bias_c)
    for k, out in enumerate((grad_b_one, grad_b_two)):
        for c in range(hidden // 128):
            at = k * (hidden // 128) + c
            out[:, pl.ds(c * 128, 128)] = biases[at : at + 1]
    wait_for(all_but_one(full_p1), recv_w.at[7])
    join_pieces(full_p1, grad_w_one)

    for k, buf in ((0, gz_x), (2, gz_a)):
        wait_for(buf.at[pl.ds(0, nrow - 1)], ssem.at[k])
    for k, buf in ((0, gx_x), (2, gx_a)):
        wait_for(buf.at[pl.ds(0, nrow - 1)], ssem.at[k])
    wait_for(all_but_one(part_one), ssem.at[1])
    wait_for(all_but_one(part_two), ssem.at[3])
    wait_for(back.at[pl.ds(0, (ncol - 1) * 128)], ssem.at[4])
    for k, buf in enumerate(
        (piece_two, z_p2, piece_one, bias_z, full_p2, z_p1, bias_x, full_p1, bias_c)
    ):
        wait_for(all_but_one(buf), ssem.at[5 + k])


def hand_over(*refs):
    count = len(refs) // 2
    for src, dst in zip(refs[:count], refs[count:], strict=True):
        dst[...] = src[...]


def per_device(
    mesh_shape,
    features, upstream, tile_values, tile_rows, tile_cols, tile_count, w_one, b_one, w_two, b_two,
):
    nz, nx, ncol = mesh_shape
    nrow = nz * nx
    slots = tile_values.shape[2]
    width = features.shape[1]
    hidden = w_one.shape[1]
    ngroup = nx * ncol
    vmem = pl.BlockSpec(memory_space=pltpu.VMEM)
    anywhere = pl.BlockSpec(memory_space=pl.ANY)
    per_one = width * hidden // (8 * 128) // ngroup * 8
    per_two = hidden * hidden // (8 * 128) // ngroup * 8
    scratch = [
        pltpu.VMEM((slots + 1, 128, 128), BF),
        pltpu.VMEM((nz, ncol * 128, nx * 128), BF),
        pltpu.VMEM((nz, nx * 128, ncol * 128), BF),
        pltpu.VMEM((nrow, 96, width), BF),
        pltpu.VMEM((nrow, 32, width), BF),
        pltpu.VMEM((nrow, 96, width), BF),
        pltpu.VMEM((nrow, 32, width), BF),
        pltpu.VMEM((nz, width, nx * 128), BF),
        pltpu.VMEM((nz, nx * 128, hidden), F32),
        pltpu.VMEM((nx * 128, hidden), BF),
        pltpu.VMEM((ncol, 128, width), F32),
        pltpu.VMEM((ncol, 128, hidden), F32),
        pltpu.VMEM((ncol, 128, width), BF),
        pltpu.VMEM((ncol, 128, width), BF),
        pltpu.VMEM((ncol, 128, hidden), BF),
        pltpu.VMEM((ncol, 128, hidden), BF),
        pltpu.VMEM((ncol * 128, hidden), BF),
        pltpu.VMEM((nx * 128, hidden), BF),
        pltpu.VMEM((ngroup, per_one, 128), F32),
        pltpu.VMEM((ngroup, per_one, 128), F32),
        pltpu.VMEM((nz, per_one, 128), F32),
        pltpu.VMEM((ngroup, per_one, 128), F32),
        pltpu.VMEM((ngroup, per_two, 128), BF),
        pltpu.VMEM((ngroup, per_two, 128), BF),
        pltpu.VMEM((nz, per_two, 128), F32),
        pltpu.VMEM((ngroup, per_two, 128), F32),
        pltpu.VMEM((ncol, 8, 128), F32),
        pltpu.VMEM((nx, 8, 128), F32),
        pltpu.VMEM((nz, 8, 128), F32),
        pltpu.VMEM((width, hidden), F32),
        pltpu.VMEM((8, hidden), F32),
        pltpu.VMEM((128, hidden), BF),
        pltpu.VMEM((hidden // 128, 128, 128), BF),
        pltpu.VMEM((128, hidden), BF),
        pltpu.VMEM((hidden // 128, 128, hidden), F32),
        pltpu.VMEM((128, hidden), BF),
        pltpu.VMEM((width, hidden), BF),
        pltpu.VMEM((1, hidden), F32),
        pltpu.VMEM((hidden, hidden), BF),
        pltpu.VMEM((1, hidden), F32),
        pltpu.VMEM((1, slots), jnp.int32),
        pltpu.VMEM((1, slots), jnp.int32),
        pltpu.VMEM((8, ncol * nrow), jnp.int32),
        pltpu.SMEM((8, ncol * nrow), jnp.int32),
        pltpu.SemaphoreType.DMA,
        pltpu.SemaphoreType.DMA((9,)),
        pltpu.SemaphoreType.DMA((14,)),
        pltpu.SemaphoreType.DMA((2, nrow)),
        pltpu.SemaphoreType.DMA((2, nrow)),
        pltpu.SemaphoreType.DMA((2,)),
        pltpu.SemaphoreType.DMA,
        pltpu.SemaphoreType.DMA((9,)),
    ]
    out = pl.pallas_call(
        functools.partial(kernel, nz, nx, ncol),
        out_shape=(
            jax.ShapeDtypeStruct((128, hidden), BF),
            jax.ShapeDtypeStruct((width, hidden), F32),
            jax.ShapeDtypeStruct((1, hidden), F32),
            jax.ShapeDtypeStruct((hidden, hidden), F32),
            jax.ShapeDtypeStruct((1, hidden), F32),
        ),
        in_specs=[
            pl.BlockSpec(memory_space=pltpu.SMEM), *([anywhere] * 9),
        ],
        out_specs=(vmem,) * 5,
        scratch_shapes=scratch,
        compiler_params=pltpu.CompilerParams(
            collective_id=0, has_side_effects=True, vmem_limit_bytes=56 * 1024 * 1024
        ),
    )(
        tile_count, features, upstream, tile_values, tile_rows, tile_cols,
        w_one, b_one.reshape(1, hidden), w_two, b_two.reshape(1, hidden),
    )
    hidden_out, grad_w_one, grad_b_one, grad_w_two, grad_b_two = pl.pallas_call(
        hand_over,
        out_shape=tuple(jax.ShapeDtypeStruct(o.shape, o.dtype) for o in out),
        in_specs=[vmem] * 5,
        out_specs=(vmem,) * 5,
    )(*out)
    return (
        hidden_out, grad_w_one, grad_b_one.reshape(hidden), grad_w_two, grad_b_two.reshape(hidden)
    )


def solution(mesh, nx=4):
    nrow, ncol = mesh.shape["row"], mesh.shape["col"]
    in_specs = (
        P(("col", "row"), None),
        P(("col", "row"), None),
        P("row", "col", None, None, None),
        P("row", "col", None),
        P("row", "col", None),
        P("row", "col"),
        P(),
        P(),
        P(),
        P(),
    )
    out_specs = (P(("col", "row"), None), P(), P(), P(), P())
    return jax.shard_map(
        functools.partial(per_device, (nrow // nx, nx, ncol)),
        mesh=mesh, in_specs=in_specs, out_specs=out_specs, check_vma=False,
    )
```

time: 121 us -> 89.1 us (0.74)
  Pallas kernels: 110 us -> 87.7 us
  local copies, waits for them, and re-layouts: 7.19 us -> 0 us
  other arithmetic: 1.41 us -> 0 us
    pallas_call x1, Pallas kernels: 110 us -> 85.9 us  [per_device(): pl.pallas_call(functools.partial(kernel, nz, nx, ncol), out_shape=(jax.Sh...]
    unnamed x5 -> x0, local copies, waits for them, and re-layouts: 7.19 us -> none
    pallas_call x0 -> x1, Pallas kernels: none -> 1.8 us  [per_device(): pl.pallas_call(hand_over, out_shape=tuple((jax.ShapeDtypeStruct(o.shape,...]
    add x2 -> x0, other arithmetic: 1.27 us -> none  [the longest x1 0.7 us: per_device(): tile_rows[0, 0] * nrow + tile_cols[0, 0]]
where the time goes in v2:
time: 89.1 us; the launch traced here: 89 us
  Pallas kernels  87.7 us (98%)
  between operations  1.29 us (1%)
    pallas_call x1, Pallas kernels, per_device(): pl.pallas_call(functools.partial(kernel, nz, nx, ncol), out_shape=(jax.Sh...  85.9 us
    pallas_call x1, Pallas kernels, per_device(): pl.pallas_call(hand_over, out_shape=tuple((jax.ShapeDtypeStruct(o.shape,...  1.8 us

profile of v2, /device:TPU:1, one launch (start us, length us, event | category | flops | bytes accessed | tf_op | source)
XLA Modules:
  0.0 89.0 jit_solution(12468484482796895970)
XLA Ops:
  1.3 85.9 %shard_map.137 = (bf16[128,256]{1,0:T(8,128)(2,1)}, f32[128,256]{1,0:T(8,128)}, f32[1,256]{1,0:T(1,128)}, f32[256,256]{1,0:T(8,128)}, f32[1,256]{1,0:T(1,128)}) custom-call(s32[1,1]{1,0:T(1,128)S(6)} %copy.15.count, bf16[128,128]{1,0:T(8,128)(2,1)} %features.1, bf16[128,256]{1,0:T(8,128)(2,1)} %upstream_hbm.1, bf16[1,1,192,128,128]{4,3,2,1,0:T(8,128)(2,1)} %tiles_hbm.1, ...), custom_call_target="tpu_custom_call" | custom-call | tf_op jit(solution)/shard_map/pallas_call | solution.py:497
  87.2 1.8 %shard_map.138 = (bf16[128,256]{1,0:T(8,128)(2,1)}, f32[128,256]{1,0:T(8,128)}, f32[1,256]{1,0:T(1,128)}, f32[256,256]{1,0:T(8,128)}, f32[1,256]{1,0:T(1,128)}) custom-call(bf16[128,256]{1,0:T(8,128)(2,1)} %get-tuple-element.15.refs_0_, f32[128,256]{1,0:T(8,128)} %get-tuple-element.16.refs_1_, f32[1,256]{1,0:T(1,128)} %get-tuple-element.17.refs_2_, ...), custom_call_target="tpu_custom_call" | custom-call | tf_op jit(solution)/shard_map/pallas_call | solution.py:518

commit v3 on v2

--- a/solution.py
+++ b/solution.py
@@ -77,7 +77,6 @@
     ]
     for copy in own_copies:
         copy.start()
-    tile_copy.start()
 
     barrier = pltpu.get_barrier_semaphore()
 
@@ -89,6 +88,12 @@
     def _(d):
         pl.semaphore_signal(
             barrier, inc=1, device_id={"row": lax.rem(mz + d, nz) * nx + mx}, device_id_type=MESH
+        )
+
+    @pl.loop(1, nrow)
+    def _(d):
+        pl.semaphore_signal(
+            barrier, inc=1, device_id={"row": lax.rem(row + d, nrow)}, device_id_type=MESH
         )
 
     @pl.loop(1, ngroup)
@@ -132,21 +137,27 @@
                 push(by_z, sems_z, at, 1, mz, peer_x(e))
 
         def use(d):
-            for e in range(1, nx):
-                arrived(by_z, sems_z, peer_z(d) * nx + peer_x(e), 1)
-            if d:
-                arrived(by_x, sems_x, peer_z(d) * nx, nx)
-            compute(peer_z(d))
-
-        between()
+            zp = peer_z(d)
+
+            @pl.loop(1, nx)
+            def _(e):
+                arrived(by_z, sems_z, zp * nx + peer_x(e), 1)
+
+            compute(zp)
+
         near_first = far_first[::-1]
         early = len(near_first) // 2 + 1
         for d in near_first[:early]:
             onward(d)
+        between()
         use(0)
         for d in near_first[early:]:
             onward(d)
-        for d in near_first:
+
+        @pl.loop(1, nz)
+        def _(q):
+            d = ((q + 1) // 2) * (2 * lax.rem(q, 2) - 1)
+            arrived(by_x, sems_x, peer_z(d) * nx, nx)
             use(d)
 
     def scatter_col(acc, part, land, rsem, ssem_):
@@ -164,8 +175,13 @@
         return total.astype(BF)
 
     def own_placed():
+        tile_copy.start()
+        find_slots()
         own_copies[2].wait()
         own_copies[3].wait()
+
+    def to_smem():
+        return pltpu.make_async_copy(slots_vmem, slot_of, in_sem.at[0])
 
     def find_slots():
         own_copies[0].wait()
@@ -178,14 +194,15 @@
         entry = lax.broadcasted_iota(jnp.int32, (slots, places), 0) - slots
         found = jnp.sum(jnp.where(hit, entry, 0), axis=0, keepdims=True) + slots
         slots_vmem[...] = jnp.broadcast_to(found, slots_vmem.shape)
-        to_smem = pltpu.make_async_copy(slots_vmem, slot_of, in_sem.at[0])
-        to_smem.start()
+        to_smem().start()
         tiles[slots] = jnp.zeros(tiles.shape[1:], BF)
         acc_one[...] = jnp.zeros(acc_one.shape, F32)
         acc_two[...] = jnp.zeros(acc_two.shape, F32)
+
+    def find_done():
         for copy in own_copies[4:]:
             copy.wait()
-        to_smem.wait()
+        to_smem().wait()
         tile_copy.wait()
 
     def build_dense(zp):
@@ -229,11 +246,11 @@
         by_z[row] = value[:cut]
         by_x[row] = value[cut:]
 
-    pl.semaphore_wait(barrier, nz - 1 + ngroup - 1)
+    pl.semaphore_wait(barrier, nz - 1 + ngroup - 1 + nrow - 1)
 
     gather_row(
         gz_x, gx_x, features.at[pl.ds(0, cut)], features.at[pl.ds(cut, 128 - cut)],
-        recv_x, ssem.at[0], layer_one, own_placed, find_slots,
+        recv_x, ssem.at[0], layer_one, own_placed, find_done,
     )
 
 
@@ -254,6 +271,12 @@
         lambda: None, lambda: None,
     )
 
+
+    my_y = col // 2
+    core = lax.rem(col, 2)
+    sibling = 1 - core
+    twin = my_y * 2 + sibling
+    ny = ncol // 2
 
     scatter_col(acc_two, part_two, land_two, recv_c.at[1], ssem.at[3])
 
@@ -277,11 +300,15 @@
             grad, w_two[...], (((1,), (1,)), ((), ())), preferred_element_type=F32
         ).astype(BF)
 
-    own_back = back.at[pl.ds(pl.multiple_of(col * 128, 128), 128)]
-
-    @pl.loop(1, ncol)
-    def _(d):
-        send(own_back, own_back, ssem.at[4], recv_back, col=lax.rem(col + d, ncol))
+    def back_of(c):
+        return back.at[pl.ds(pl.multiple_of(c * 128, 128), 128)]
+
+    for d in range(1, ny):
+        send(
+            back_of(col), back_of(col), ssem.at[4], recv_back.at[col],
+            col=2 * lax.rem(my_y + d, ny) + core,
+        )
+    send(back_of(col), back_of(col), ssem.at[4], recv_back.at[col], col=twin)
 
     for m in range(hidden // 128):
         agg_ht[m] = agg_h[:, m * 128 : m * 128 + 128].T
@@ -346,21 +373,26 @@
         return buf.at[pl.ds(0, buf.shape[0] - 1)]
 
     split_pieces(piece_two, local_w_two)
+    for d in (1, 3, 2) if ny == 4 else range(1, ny):
+        c = 2 * lax.rem(my_y + d, ny) + core
+        wait_for(back_of(c), recv_back.at[c])
+        send(back_of(c), back_of(c), ssem.at[14], recv_back.at[c], col=twin)
     spread_group(piece_two, land_p2, ssem.at[5], recv_w.at[0])
-
-    wait_for(back.at[pl.ds(0, (ncol - 1) * 128)], recv_back)
+    for d in range(ny):
+        c = 2 * lax.rem(my_y + d, ny) + sibling
+        wait_for(back_of(c), recv_back.at[c])
 
     def backward(first, last):
-        @pl.loop(first, last)
+        @pl.loop(first, last, step=2)
         def _(zp):
-            for p in range(1):
-                at = pl.ds(0, nx * 128)
-                grad_one = (matmul(dense_t[zp, at], back[...]) * slope[zp, at]).astype(BF)
-                gone[at] = grad_one
+            for k in range(2):
+                grad_one = (matmul(dense_t[zp + k], back[...]) * slope[zp + k]).astype(BF)
+                gone[k] = grad_one
                 acc_b[...] = acc_b[...] + jnp.sum(
                     grad_one.astype(F32).reshape(nx * 16, 8, hidden), axis=0
                 )
-            acc_w[...] = acc_w[...] + matmul(agg_t[zp], gone[...])
+            for k in range(2):
+                acc_w[...] = acc_w[...] + matmul(agg_t[zp + k], gone[k])
 
     acc_w[...] = jnp.zeros(acc_w.shape, F32)
     acc_b[...] = jnp.zeros(acc_b.shape, F32)
@@ -413,7 +445,8 @@
         wait_for(buf.at[pl.ds(0, nrow - 1)], ssem.at[k])
     wait_for(all_but_one(part_one), ssem.at[1])
     wait_for(all_but_one(part_two), ssem.at[3])
-    wait_for(back.at[pl.ds(0, (ncol - 1) * 128)], ssem.at[4])
+    wait_for(back.at[pl.ds(0, ny * 128)], ssem.at[4])
+    wait_for(back.at[pl.ds(0, (ny - 1) * 128)], ssem.at[14])
     for k, buf in enumerate(
         (piece_two, z_p2, piece_one, bias_z, full_p2, z_p1, bias_x, full_p1, bias_c)
     ):
@@ -458,7 +491,7 @@
         pltpu.VMEM((ncol, 128, hidden), BF),
         pltpu.VMEM((ncol, 128, hidden), BF),
         pltpu.VMEM((ncol * 128, hidden), BF),
-        pltpu.VMEM((nx * 128, hidden), BF),
+        pltpu.VMEM((2, nx * 128, hidden), BF),
         pltpu.VMEM((ngroup, per_one, 128), F32),
         pltpu.VMEM((ngroup, per_one, 128), F32),
         pltpu.VMEM((nz, per_one, 128), F32),
@@ -487,11 +520,11 @@
         pltpu.SMEM((8, ncol * nrow), jnp.int32),
         pltpu.SemaphoreType.DMA,
         pltpu.SemaphoreType.DMA((9,)),
-        pltpu.SemaphoreType.DMA((14,)),
+        pltpu.SemaphoreType.DMA((15,)),
         pltpu.SemaphoreType.DMA((2, nrow)),
         pltpu.SemaphoreType.DMA((2, nrow)),
         pltpu.SemaphoreType.DMA((2,)),
-        pltpu.SemaphoreType.DMA,
+        pltpu.SemaphoreType.DMA((ncol,)),
         pltpu.SemaphoreType.DMA((9,)),
     ]
     out = pl.pallas_call(

time: 89.1 us -> 86.2 us (0.967)
  Pallas kernels: 87.7 us -> 84.8 us
    pallas_call x1, Pallas kernels: 85.9 us -> 83 us  [per_device(): pl.pallas_call(functools.partial(kernel, nz, nx, ncol), out_shape=(jax.Sh...]
where the time goes in v3:
time: 86.2 us; the launch traced here: 86.1 us
  Pallas kernels  84.8 us (98%)
  between operations  1.29 us (1%)
    pallas_call x1, Pallas kernels, per_device(): pl.pallas_call(functools.partial(kernel, nz, nx, ncol), out_shape=(jax.Sh...  83 us
    pallas_call x1, Pallas kernels, per_device(): pl.pallas_call(hand_over, out_shape=tuple((jax.ShapeDtypeStruct(o.shape,...  1.8 us

profile of v3, /device:TPU:1, one launch (start us, length us, event | category | flops | bytes accessed | tf_op | source)
XLA Modules:
  0.0 86.1 jit_solution(3448013491152325686)
XLA Ops:
  1.3 83.0 %shard_map.137 = (bf16[128,256]{1,0:T(8,128)(2,1)}, f32[128,256]{1,0:T(8,128)}, f32[1,256]{1,0:T(1,128)}, f32[256,256]{1,0:T(8,128)}, f32[1,256]{1,0:T(1,128)}) custom-call(s32[1,1]{1,0:T(1,128)S(6)} %copy.15.count, bf16[128,128]{1,0:T(8,128)(2,1)} %features.1, bf16[128,256]{1,0:T(8,128)(2,1)} %upstream_hbm.1, bf16[1,1,192,128,128]{4,3,2,1,0:T(8,128)(2,1)} %tiles_hbm.1, ...), custom_call_target="tpu_custom_call" | custom-call | tf_op jit(solution)/shard_map/pallas_call | solution.py:530
  84.3 1.8 %shard_map.138 = (bf16[128,256]{1,0:T(8,128)(2,1)}, f32[128,256]{1,0:T(8,128)}, f32[1,256]{1,0:T(1,128)}, f32[256,256]{1,0:T(8,128)}, f32[1,256]{1,0:T(1,128)}) custom-call(bf16[128,256]{1,0:T(8,128)(2,1)} %get-tuple-element.15.refs_0_, f32[128,256]{1,0:T(8,128)} %get-tuple-element.16.refs_1_, f32[1,256]{1,0:T(1,128)} %get-tuple-element.17.refs_2_, ...), custom_call_target="tpu_custom_call" | custom-call | tf_op jit(solution)/shard_map/pallas_call | solution.py:551

commit v4 on v3

--- a/solution.py
+++ b/solution.py
@@ -160,10 +160,19 @@
             arrived(by_x, sems_x, peer_z(d) * nx, nx)
             use(d)
 
+    my_y = col // 2
+    core = lax.rem(col, 2)
+    ny = ncol // 2
+    steps_y = sorted(range(1, ny), key=lambda d: -min(d, ny - d))
+    col_order = [(d, c) for d in steps_y for c in (0, 1)] + [(0, 1)]
+
+    def col_peer(d):
+        other = core if d[1] == 0 else 1 - core
+        return 2 * lax.rem(my_y + d[0], ny) + other
+
     def scatter_col(acc, part, land, rsem, ssem_):
-        @pl.loop(1, ncol)
-        def _(d):
-            to = lax.rem(col + d, ncol)
+        for d in col_order:
+            to = col_peer(d)
             part[to] = acc[to].astype(BF)
             send(part.at[to], land.at[col], ssem_, rsem, col=to)
 
@@ -272,12 +281,6 @@
     )
 
 
-    my_y = col // 2
-    core = lax.rem(col, 2)
-    sibling = 1 - core
-    twin = my_y * 2 + sibling
-    ny = ncol // 2
-
     scatter_col(acc_two, part_two, land_two, recv_c.at[1], ssem.at[3])
 
     @pl.loop(0, nz)
@@ -288,27 +291,23 @@
 
     agg_h[...] = scattered_col(acc_two, land_two, recv_c.at[1])
 
-    @pl.loop(0, 2)
+    @pl.loop(0, 1)
     def _(m):
-        at = pl.ds(pl.multiple_of(m * 64, 64), 64)
+        at = pl.ds(pl.multiple_of(m * 128, 128), 128)
         pre = matmul(agg_h[at], w_two[...]) + b_two[...]
         sig = jax.nn.sigmoid(pre)
         hidden_out[at] = (pre * sig).astype(BF)
         grad = (upstream[at].astype(F32) * dsilu_from(pre, sig)).astype(BF)
         grad_h[at] = grad
-        back[pl.ds(pl.multiple_of(col * 128 + m * 64, 64), 64)] = lax.dot_general(
+        back[pl.ds(pl.multiple_of((col + m) * 128, 128), 128)] = lax.dot_general(
             grad, w_two[...], (((1,), (1,)), ((), ())), preferred_element_type=F32
         ).astype(BF)
 
     def back_of(c):
         return back.at[pl.ds(pl.multiple_of(c * 128, 128), 128)]
 
-    for d in range(1, ny):
-        send(
-            back_of(col), back_of(col), ssem.at[4], recv_back.at[col],
-            col=2 * lax.rem(my_y + d, ny) + core,
-        )
-    send(back_of(col), back_of(col), ssem.at[4], recv_back.at[col], col=twin)
+    for d in col_order:
+        send(back_of(col), back_of(col), ssem.at[4], recv_back.at[0], col=col_peer(d))
 
     for m in range(hidden // 128):
         agg_ht[m] = agg_h[:, m * 128 : m * 128 + 128].T
@@ -373,25 +372,21 @@
         return buf.at[pl.ds(0, buf.shape[0] - 1)]
 
     split_pieces(piece_two, local_w_two)
-    for d in (1, 3, 2) if ny == 4 else range(1, ny):
-        c = 2 * lax.rem(my_y + d, ny) + core
-        wait_for(back_of(c), recv_back.at[c])
-        send(back_of(c), back_of(c), ssem.at[14], recv_back.at[c], col=twin)
     spread_group(piece_two, land_p2, ssem.at[5], recv_w.at[0])
-    for d in range(ny):
-        c = 2 * lax.rem(my_y + d, ny) + sibling
-        wait_for(back_of(c), recv_back.at[c])
+    wait_for(back.at[pl.ds(0, (ncol - 1) * 128)], recv_back.at[0])
+
+    per_step = gone.shape[0]
 
     def backward(first, last):
-        @pl.loop(first, last, step=2)
+        @pl.loop(first, last, step=per_step)
         def _(zp):
-            for k in range(2):
+            for k in range(per_step):
                 grad_one = (matmul(dense_t[zp + k], back[...]) * slope[zp + k]).astype(BF)
                 gone[k] = grad_one
                 acc_b[...] = acc_b[...] + jnp.sum(
                     grad_one.astype(F32).reshape(nx * 16, 8, hidden), axis=0
                 )
-            for k in range(2):
+            for k in range(per_step):
                 acc_w[...] = acc_w[...] + matmul(agg_t[zp + k], gone[k])
 
     acc_w[...] = jnp.zeros(acc_w.shape, F32)
@@ -445,8 +440,7 @@
         wait_for(buf.at[pl.ds(0, nrow - 1)], ssem.at[k])
     wait_for(all_but_one(part_one), ssem.at[1])
     wait_for(all_but_one(part_two), ssem.at[3])
-    wait_for(back.at[pl.ds(0, ny * 128)], ssem.at[4])
-    wait_for(back.at[pl.ds(0, (ny - 1) * 128)], ssem.at[14])
+    wait_for(back.at[pl.ds(0, (ncol - 1) * 128)], ssem.at[4])
     for k, buf in enumerate(
         (piece_two, z_p2, piece_one, bias_z, full_p2, z_p1, bias_x, full_p1, bias_c)
     ):
@@ -491,7 +485,7 @@
         pltpu.VMEM((ncol, 128, hidden), BF),
         pltpu.VMEM((ncol, 128, hidden), BF),
         pltpu.VMEM((ncol * 128, hidden), BF),
-        pltpu.VMEM((2, nx * 128, hidden), BF),
+        pltpu.VMEM((nz // 2, nx * 128, hidden), BF),
         pltpu.VMEM((ngroup, per_one, 128), F32),
         pltpu.VMEM((ngroup, per_one, 128), F32),
         pltpu.VMEM((nz, per_one, 128), F32),

time: 86.2 us -> 84.9 us (0.985)
  Pallas kernels: 84.8 us -> 83.5 us
    pallas_call x1, Pallas kernels: 83 us -> 81.7 us  [per_device(): pl.pallas_call(functools.partial(kernel, nz, nx, ncol), out_shape=(jax.Sh...]
where the time goes in v4:
time: 84.9 us; the launch traced here: 84.8 us
  Pallas kernels  83.5 us (98%)
  between operations  1.29 us (2%)
    pallas_call x1, Pallas kernels, per_device(): pl.pallas_call(functools.partial(kernel, nz, nx, ncol), out_shape=(jax.Sh...  81.7 us
    pallas_call x1, Pallas kernels, per_device(): pl.pallas_call(hand_over, out_shape=tuple((jax.ShapeDtypeStruct(o.shape,...  1.8 us

profile of v4, /device:TPU:1, one launch (start us, length us, event | category | flops | bytes accessed | tf_op | source)
XLA Modules:
  0.0 84.8 jit_solution(10677635475221132560)
XLA Ops:
  1.3 81.7 %shard_map.137 = (bf16[128,256]{1,0:T(8,128)(2,1)}, f32[128,256]{1,0:T(8,128)}, f32[1,256]{1,0:T(1,128)}, f32[256,256]{1,0:T(8,128)}, f32[1,256]{1,0:T(1,128)}) custom-call(s32[1,1]{1,0:T(1,128)S(6)} %copy.15.count, bf16[128,128]{1,0:T(8,128)(2,1)} %features.1, bf16[128,256]{1,0:T(8,128)(2,1)} %upstream_hbm.1, bf16[1,1,192,128,128]{4,3,2,1,0:T(8,128)(2,1)} %tiles_hbm.1, ...), custom_call_target="tpu_custom_call" | custom-call | tf_op jit(solution)/shard_map/pallas_call | solution.py:524
  83.0 1.8 %shard_map.138 = (bf16[128,256]{1,0:T(8,128)(2,1)}, f32[128,256]{1,0:T(8,128)}, f32[1,256]{1,0:T(1,128)}, f32[256,256]{1,0:T(8,128)}, f32[1,256]{1,0:T(1,128)}) custom-call(bf16[128,256]{1,0:T(8,128)(2,1)} %get-tuple-element.15.refs_0_, f32[128,256]{1,0:T(8,128)} %get-tuple-element.16.refs_1_, f32[1,256]{1,0:T(1,128)} %get-tuple-element.17.refs_2_, ...), custom_call_target="tpu_custom_call" | custom-call | tf_op jit(solution)/shard_map/pallas_call | solution.py:545

commit v5 on v4

--- a/solution.py
+++ b/solution.py
@@ -146,13 +146,10 @@
             compute(zp)
 
         near_first = far_first[::-1]
-        early = len(near_first) // 2 + 1
-        for d in near_first[:early]:
+        for d in near_first:
             onward(d)
         between()
         use(0)
-        for d in near_first[early:]:
-            onward(d)
 
         @pl.loop(1, nz)
         def _(q):

time: 84.9 us -> 84.9 us (level)
  no operation moved by 1% of the time
where the time goes in v5:
time: 84.9 us; the launch traced here: 84.8 us
  Pallas kernels  83.5 us (98%)
  between operations  1.29 us (2%)
    pallas_call x1, Pallas kernels, per_device(): pl.pallas_call(functools.partial(kernel, nz, nx, ncol), out_shape=(jax.Sh...  81.7 us
    pallas_call x1, Pallas kernels, per_device(): pl.pallas_call(hand_over, out_shape=tuple((jax.ShapeDtypeStruct(o.shape,...  1.8 us

profile of v5, /device:TPU:1, one launch (start us, length us, event | category | flops | bytes accessed | tf_op | source)
XLA Modules:
  0.0 84.8 jit_solution(18393648011228313047)
XLA Ops:
  1.3 81.7 %shard_map.137 = (bf16[128,256]{1,0:T(8,128)(2,1)}, f32[128,256]{1,0:T(8,128)}, f32[1,256]{1,0:T(1,128)}, f32[256,256]{1,0:T(8,128)}, f32[1,256]{1,0:T(1,128)}) custom-call(s32[1,1]{1,0:T(1,128)S(6)} %copy.15.count, bf16[128,128]{1,0:T(8,128)(2,1)} %features.1, bf16[128,256]{1,0:T(8,128)(2,1)} %upstream_hbm.1, bf16[1,1,192,128,128]{4,3,2,1,0:T(8,128)(2,1)} %tiles_hbm.1, ...), custom_call_target="tpu_custom_call" | custom-call | tf_op jit(solution)/shard_map/pallas_call | solution.py:521
  83.0 1.8 %shard_map.138 = (bf16[128,256]{1,0:T(8,128)(2,1)}, f32[128,256]{1,0:T(8,128)}, f32[1,256]{1,0:T(1,128)}, f32[256,256]{1,0:T(8,128)}, f32[1,256]{1,0:T(1,128)}) custom-call(bf16[128,256]{1,0:T(8,128)(2,1)} %get-tuple-element.15.refs_0_, f32[128,256]{1,0:T(8,128)} %get-tuple-element.16.refs_1_, f32[1,256]{1,0:T(1,128)} %get-tuple-element.17.refs_2_, ...), custom_call_target="tpu_custom_call" | custom-call | tf_op jit(solution)/shard_map/pallas_call | solution.py:542
